TPU v7x, 512 devices: a whole 4x8x8 slice. The times are simulated.
512 devices in a mesh: scen: 16 (over y, core), fac: 32 (over z, x).
Axes of the slice: x: 4, y: 8, z: 8, core: 2. Of those that a mesh axis runs over, the one named last changes fastest.
Arguments:
- shocks: bfloat16 [2, 4096, 256], P(None, 'scen'), may hold values from -6 to 6
- loadings: bfloat16 [256, 8192], P(None, 'fac'), may hold values from -0.375 to 0.375
- vol: float32 [8192], P('fac'), may hold values from 0.1 to 0.5
- jump_counts: int32 [2, 4096, 8192], P(None, 'scen', 'fac'), may hold values from 0 to 3
- jump_noise: bfloat16 [2, 4096, 8192], P(None, 'scen', 'fac'), may hold values from -6 to 6
- jump_mean: float32 [8192], P('fac'), may hold values from -0.15 to 0.1
- jump_vol: float32 [8192], P('fac'), may hold values from 0.05 to 0.3
- dependencies: int32 [8192, 2], P('fac'), may hold values from 0 to 63, as said below
- block_slot: int32 [64], replicated, may hold values from 0 to 63, each once
- trade_weights: bfloat16 [8192, 2, 128], P('fac'), may hold values from -0.375 to 0.375
- netting: int32 [8192], P('fac'), may hold values from 0 to 2047
Outputs:
- exposure: float32 [2, 2048, 4096], P(None, 'fac', 'scen')
- expected: float32 [2, 2048], P(None, 'fac')
Inputs may be any that keep to these rules, and one draw needn't show every extreme that they name: `dependencies`: each trade names 2 different blocks.
All inputs are finite; a program needn't handle non-finite values.
Results may differ from a plain program's by a relative error of at most 0.0056.
Values may be sent and summed in bfloat16 or wider, within the bound.
A program may use at most 192 MiB of HBM per device.

v0:
```python
import jax
import jax.numpy as jnp
from jax import lax
from jax.sharding import PartitionSpec as P

BLOCK = 128
SET_DEV = 64
DATES = 2


def body(
    shocks,
    loadings,
    vol,
    jump_counts,
    jump_noise,
    jump_mean,
    jump_vol,
    dependencies,
    block_slot,
    trade_weights,
    netting,
):
    fac_count = lax.axis_size("fac")
    scen_count = lax.axis_size("scen")
    rows = shocks.shape[1]
    fac_width = loadings.shape[1]
    factors = fac_width * fac_count
    nblocks = factors // BLOCK
    trade_count = trade_weights.shape[0]
    set_total = SET_DEV * fac_count
    slots = block_slot[dependencies]
    marks = (slots[:, :, None] == jnp.arange(nblocks, dtype=jnp.int32)[None, None, :]).astype(
        jnp.bfloat16
    )
    dense = jnp.einsum("tkb,tkj->bjt", marks, trade_weights, preferred_element_type=jnp.float32)
    dense = dense.astype(jnp.bfloat16).reshape(factors, trade_count)
    level = jnp.zeros((rows, fac_width), jnp.float32)
    exposures = []
    totals = []
    for date in range(DATES):
        diffuse = jnp.dot(shocks[date], loadings, preferred_element_type=jnp.float32)
        counts = jump_counts[date].astype(jnp.float32)
        level = (
            level
            + vol * diffuse
            - 0.5 * vol * vol
            + counts * jump_mean
            + jnp.sqrt(counts) * jump_vol * jump_noise[date].astype(jnp.float32)
        )
        prices = (jnp.exp(level) - 1.0).astype(jnp.bfloat16)
        values = jnp.dot(
            lax.all_gather(prices, "fac", axis=1, tiled=True),
            dense,
            preferred_element_type=jnp.float32,
        )
        partial_value = jax.ops.segment_sum(values.T, netting, num_segments=set_total)
        nets = lax.psum_scatter(partial_value, "fac", scatter_dimension=0, tiled=True)
        exposure = jnp.maximum(nets, 0.0)
        exposures.append(exposure)
        totals.append(jnp.sum(exposure, axis=1))
    summed = lax.psum(jnp.stack(totals), "scen")
    return (jnp.stack(exposures), summed / (rows * scen_count))


def solution(mesh):
    placed = (
        P(None, "scen", None),
        P(None, "fac"),
        P("fac"),
        P(None, "scen", "fac"),
        P(None, "scen", "fac"),
        P("fac"),
        P("fac"),
        P("fac", None),
        P(),
        P("fac", None, None),
        P("fac"),
    )
    return jax.shard_map(
        body,
        mesh=mesh,
        in_specs=placed,
        out_specs=(P(None, "fac", "scen"), P(None, "fac")),
        check_vma=False,
    )
```

profile of v0, /device:TPU:1, one launch (start us, length us, event | category | flops | bytes accessed | tf_op | source)
XLA Modules:
  0.0 684.2 jit_solution(10813429482090959501)
XLA Ops:
  7.2 0.7 multiply_multiply_fusion
  7.9 2.1 add_convert_fusion
  10.0 2.1 fusion.15
  12.1 0.7 all-gather.3.cloned.1.call-update
  12.9 0.7 compare_select_fusion
  13.6 0.1 copy.13
  13.7 0.1 reshape.23
  13.9 3.3 gather_fusion
  17.3 0.1 reshape.22
  17.4 4.3 convolution_convert_fusion
  21.7 82.4 %all-gather.5.cloned.1.call-done = bf16[256,8192]{1,0:T(8,128)(2,1)} async-done(((bf16[256,256]{1,0:T(8,128)(2,1)}), bf16[256,8192]{1,0:T(8,128)(2,1)}) %all-gather.5.cloned.1.call-update) | async-done | bytes 4194320 | tf_op jit(solution)/shard_map/all_gather | solution.py:53
  104.1 6.3 fusion
  110.4 3.6 scatter_custom_fusion.1
  113.9 0.0 reduce-scatter.3.cloned.1.call-start
  114.0 83.1 %all-gather.3.cloned.1.call-done = bf16[256,8192]{1,0:T(8,128)(2,1)} async-done(((bf16[256,256]{1,0:T(8,128)(2,1)}), bf16[256,8192]{1,0:T(8,128)(2,1)}) %all-gather.3.cloned.1.call-update) | async-done | bytes 4194320 | tf_op jit(solution)/shard_map/all_gather | solution.py:53
  197.1 6.3 fusion.2
  203.4 3.5 scatter_custom_fusion
  206.9 214.8 %reduce-scatter.5.cloned.1.call-done = f32[64,256]{1,0:T(8,128)} async-done(((f32[2048,256]{1,0:T(8,128)}), f32[64,256]{1,0:T(8,128)}) %reduce-scatter.5.cloned.1.call-update) | async-done | bytes 65552 | tf_op jit(solution)/shard_map/reduce_scatter | solution.py:58
  421.8 0.9 maximum_reduce_fusion
  422.7 223.9 %reduce-scatter.3.cloned.1.call-done = f32[64,256]{1,0:T(8,128)} async-done(((f32[2048,256]{1,0:T(8,128)}), f32[64,256]{1,0:T(8,128)}) %reduce-scatter.3.cloned.1.call-update) | async-done | bytes 65552 | tf_op jit(solution)/shard_map/reduce_scatter | solution.py:58
  646.6 0.9 maximum_reduce_fusion.1
  647.6 28.8 %psum.7 = f32[2,64]{1,0:T(2,128)S(1)} all-reduce(f32[2,64]{1,0:T(2,128)S(1)} %pad_maximum_fusion.1), channel_id=1, replica_groups=mesh['scen'=16,'fac'=32] {'scen'}, use_global_device_ids=true, to_apply=%region_6.0 | all-reduce | flops 128 | bytes 1024 | tf_op jit(solution)/shard_map/psum | solution.py:62
  676.4 0.6 broadcast_multiply_fusion
  677.0 0.7 pad_maximum_fusion
  (12 shorter events, 0.2 us)
Async XLA Ops:
  7.2 10.2 %copy-start = (bf16[256,2,128]{2,1,0:T(2,128)(2,1)S(1)}, bf16[256,2,128]{2,1,0:T(2,128)(2,1)}, u32[]{:S(2)}) copy-start(bf16[256,2,128]{2,1,0:T(2,128)(2,1)} %param.20) | copy-start | bytes 393220
  7.2 6.7 copy-start.1
  7.2 96.9 %all-gather.5.cloned.1.call-start = ((), (), s32[]{:S(2)}) async-start(), calls=%async_computation.4 | async-start | bytes 4325376 | tf_op jit(solution)/shard_map/all_gather | solution.py:53
  12.1 185.0 %all-gather.3.cloned.1.call-start = ((), (), s32[]{:S(2)}) async-start(), calls=%async_computation.2 | async-start | bytes 4325376 | tf_op jit(solution)/shard_map/all_gather | solution.py:53
  12.9 408.9 %reduce-scatter.5.cloned.1.call-start = ((), (), s32[]{:S(2)}) async-start(), calls=%async_computation.5 | async-start | bytes 2162688 | tf_op jit(solution)/shard_map/reduce_scatter | solution.py:58
  113.9 532.7 %reduce-scatter.3.cloned.1.call-start = ((), (), s32[]{:S(2)}) async-start(), calls=%async_computation.3 | async-start | bytes 2162688 | tf_op jit(solution)/shard_map/reduce_scatter | solution.py:58
Sparse Core Ops, SparseCore 0:
  12.2 91.8 all-gather.4
  107.7 89.3 all-gather.2
  201.5 220.2 reduce-scatter.4
  426.7 219.9 reduce-scatter.2
where the time goes:
time: 684 us
  waiting for transfers between devices  605 us (88%)
  blocking collectives  28.8 us (4%)
  matrix products  21 us (3%)
  between operations  13.9 us (2%)
  other arithmetic  11.6 us (2%)
    reduce_scatter x2, waiting for transfers between devices, body(): lax.psum_scatter(partial_value, 'fac', scatter_dimension=0, tiled=True)  439 us
    all_gather x2, waiting for transfers between devices, body(): lax.all_gather(prices, 'fac', axis=1, tiled=True)  165 us
    psum x1, blocking collectives, body(): summed = lax.psum(jnp.stack(totals), 'scen')  28.8 us
  transfers between devices with their start and end apart: 4, of which 4 were waited for; matrix products, arithmetic and copies ran while one was open for 4% of the time, Pallas kernels for 0%

commit v1 on v0

v1 whole, which is shorter than its diff:
```python
import functools

import jax
import jax.numpy as jnp
from jax import lax
from jax.experimental import pallas as pl
from jax.experimental.pallas import tpu as pltpu
from jax.sharding import PartitionSpec as P

BLOCK = 128
SETS = 64
DATES = 2
CORES = 2
XS = 4
MESH = pl.DeviceIdType.MESH
F32 = jnp.float32
BF16 = jnp.bfloat16
NT = (((1,), (1,)), ((), ()))


class Ring:
    def __init__(self, n, me, axis, device, view, send, recv):
        self.n, self.me, self.axis, self.device, self.view = n, me, axis, device, view
        self.send, self.recv = send, recv
        self.last = n // 2

    def ref(self, way, d, owner):
        half = None
        if d == self.last:
            half = 0 if way == 0 else 1
        return self.view(owner, half)

    def owner(self, way, d):
        step = -d if way == 0 else d
        return lax.rem(self.me + step + self.n, self.n)

    def copy(self, way, d, shift):
        ref = self.ref(way, d, self.owner(way, d - shift))
        to = self.owner(way, -1)
        return pltpu.make_async_remote_copy(
            src_ref=ref,
            dst_ref=ref,
            send_sem=self.send.at[way, d],
            recv_sem=self.recv.at[way, d],
            device_id={self.axis: self.device(to)},
            device_id_type=MESH,
        )

    def start(self, way, d):
        self.copy(way, d, 1).start()

    def arrived(self, way, d):
        self.copy(way, d, 0).wait_recv()

    def sent(self):
        for d in range(1, self.last + 1):
            for way in range(2):
                self.copy(way, d, 1).wait_send()


def kernel(
    fac_n,
    scen_n,
    shocks,
    loadings,
    vol,
    counts,
    noise,
    jump_mean,
    jump_vol,
    deps,
    place,
    weights,
    netting,
    expo,
    mean,
    w32,
    keys,
    wg,
    marks,
    spread,
    macc,
    mg,
    level,
    pg,
    nets,
    part,
    back,
    sums,
    z_send,
    z_recv,
    x_send,
    x_recv,
    p_send,
    p_recv,
    m_send,
    m_recv,
    c_send,
    c_recv,
    r_send,
    r_recv,
    s_send,
    s_recv,
):
    zs = fac_n // XS
    ys = scen_n // CORES
    rows = shocks.shape[1]
    width = loadings.shape[1]
    local = width // BLOCK
    trades = netting.shape[1]
    jn = BLOCK // scen_n
    blocks = XS * local
    fac = lax.axis_index("fac")
    scen = lax.axis_index("scen")
    z, x = fac // XS, lax.rem(fac, XS)
    y, c = scen // CORES, lax.rem(scen, CORES)

    dep = deps[...]
    slot = jnp.zeros_like(dep)
    for b in range(place.shape[0]):
        slot = jnp.where(dep == b, place[b], slot)
    keys[x, z, :, 0:trades] = slot[0:1]
    keys[x, z, :, trades : 2 * trades] = slot[1:2]
    keys[x, z, :, 2 * trades : 3 * trades] = netting[...]
    w32[...] = weights[...].astype(F32)
    pick = (
        lax.broadcasted_iota(jnp.int32, (jn, BLOCK), 1)
        == lax.broadcasted_iota(jnp.int32, (jn, BLOCK), 0) + scen * jn
    ).astype(F32).astype(BF16)
    chosen = [
        lax.dot_general(
            pick, w32[pl.ds(k, trades, stride=2), :].astype(BF16), NT, preferred_element_type=F32
        )
        for k in range(2)
    ]
    wg[x, z] = jnp.concatenate(chosen, axis=0).astype(BF16)

    barrier = pltpu.get_barrier_semaphore()
    partners = 0
    for d in range(1, zs):
        pl.semaphore_signal(
            barrier, inc=1, device_id={"fac": lax.rem(z + d, zs) * XS + x}, device_id_type=MESH
        )
        partners += 1
    for d in range(1, XS):
        pl.semaphore_signal(
            barrier, inc=1, device_id={"fac": z * XS + lax.rem(x + d, XS)}, device_id_type=MESH
        )
        partners += 1
    for d in range(1, scen_n):
        pl.semaphore_signal(
            barrier, inc=1, device_id={"scen": lax.rem(scen + d, scen_n)}, device_id_type=MESH
        )
        partners += 1
    pl.semaphore_wait(barrier, partners)

    def z_copy(kind, d, from_z):
        ref = keys.at[x, from_z] if kind == 0 else wg.at[x, from_z]
        return pltpu.make_async_remote_copy(
            src_ref=ref,
            dst_ref=ref,
            send_sem=z_send.at[kind, d],
            recv_sem=z_recv.at[kind, d],
            device_id={"fac": lax.rem(z + d, zs) * XS + x},
            device_id_type=MESH,
        )

    def x_copy(kind, d, from_x):
        ref = keys.at[from_x] if kind == 0 else wg.at[from_x]
        return pltpu.make_async_remote_copy(
            src_ref=ref,
            dst_ref=ref,
            send_sem=x_send.at[kind, d],
            recv_sem=x_recv.at[kind, d],
            device_id={"fac": z * XS + lax.rem(x + d, XS)},
            device_id_type=MESH,
        )

    for kind in range(2):
        for d in range(1, zs):
            z_copy(kind, d, z).start()

    col_q = lax.broadcasted_iota(jnp.int32, (width, width), 1)
    col_f = (
        lax.rem(lax.div(col_q, jn), local) * BLOCK
        + lax.div(col_q, jn * local) * jn
        + lax.rem(col_q, jn)
    )
    perm = (lax.broadcasted_iota(jnp.int32, (width, width), 0) == col_f).astype(F32).astype(BF16)
    v = vol[...]
    drift = 0.5 * v * v
    for date in range(DATES):
        diffuse = jnp.dot(shocks[date], loadings[...], preferred_element_type=F32)
        number = counts[date].astype(F32)
        change = (
            v * diffuse
            - drift
            + number * jump_mean[...]
            + jnp.sqrt(number) * jump_vol[...] * noise[date].astype(F32)
        )
        now = change if date == 0 else level[...] + change
        if date < DATES - 1:
            level[...] = now
        prices = (jnp.exp(now) - 1.0).astype(BF16)
        pg[date, x] = jnp.dot(prices, perm, preferred_element_type=F32).astype(BF16)

    p_rings = []
    for date in range(DATES):

        def p_view(owner, half, date=date):
            if half is None:
                return pg.at[date, owner]
            return pg.at[date, owner, pl.ds(half * (rows // 2), rows // 2)]

        p_rings.append(
            Ring(XS, x, "fac", lambda i: z * XS + i, p_view, p_send.at[date], p_recv.at[date])
        )

    for kind in range(2):
        for d in range(1, zs):
            z_copy(kind, d, lax.rem(z - d + zs, zs)).wait_recv()
    for kind in range(2):
        for d in (1, XS - 1, 2):
            x_copy(kind, d, x).start()
    for ring in p_rings:
        for way in range(2):
            ring.start(way, 1)

    sets = zs * SETS
    macc[...] = jnp.zeros_like(macc)

    def form(owner):
        @pl.loop(0, zs)
        def _(at):
            columns = pl.ds(pl.multiple_of(at * trades, trades), trades)
            key = keys[owner, at]
            net = key[:, 2 * trades : 3 * trades]
            group = lax.shift_right_logical(net, 6)
            line = jnp.where(
                (group & (XS - 1)) == x,
                lax.shift_right_logical(group, 2) * SETS + (net & (SETS - 1)),
                -1,
            )
            marks[:, columns] = jnp.where(
                lax.broadcasted_iota(jnp.int32, (sets, trades), 0) == line, 1.0, 0.0
            ).astype(BF16)
            w = wg[owner, at].astype(F32)
            w0, w1 = w[0:jn], w[jn : 2 * jn]
            first = key[:, 0:trades] - blocks * z
            second = key[:, trades : 2 * trades] - blocks * z
            spread[:, columns] = jnp.concatenate(
                [
                    jnp.where(first == b, w0, 0.0) + jnp.where(second == b, w1, 0.0)
                    for b in range(blocks)
                ],
                axis=0,
            ).astype(BF16)

        macc[...] += lax.dot_general(spread[...], marks[...], NT, preferred_element_type=F32)

    form(x)
    for d in (1, XS - 1, 2):
        from_x = lax.rem(x - d + XS, XS)
        for kind in range(2):
            x_copy(kind, d, from_x).wait_recv()
        form(from_x)
    mg[scen] = macc[...].astype(BF16)

    half_rows = macc.shape[0] // 2

    def m_view(core):
        def view(owner, half):
            if half is None:
                return mg.at[owner * CORES + core]
            return mg.at[owner * CORES + core, pl.ds(half * half_rows, half_rows)]

        return view

    m_ring = Ring(ys, y, "scen", lambda i: i * CORES + c, m_view(c), m_send, m_recv)
    other = 1 - c

    def c_copy(way, d, mine):
        if d == 0:
            ref = m_view(c if mine else other)(y, None)
        else:
            half = None if d < m_ring.last else way
            ref = m_view(c if mine else other)(m_ring.owner(way, d), half)
        return pltpu.make_async_remote_copy(
            src_ref=ref,
            dst_ref=ref,
            send_sem=c_send.at[way, d],
            recv_sem=c_recv.at[way, d],
            device_id={"scen": y * CORES + other},
            device_id_type=MESH,
        )

    for way in range(2):
        m_ring.start(way, 1)
    c_copy(0, 0, True).start()
    for d in range(1, XS // 2):
        for ring in p_rings:
            for way in range(2):
                ring.arrived(way, d)
                ring.start(way, d + 1)
    for d in range(1, ys // 2 + 1):
        for way in range(2):
            m_ring.arrived(way, d)
            if d < ys // 2:
                m_ring.start(way, d + 1)
            c_copy(way, d, True).start()
    for ring in p_rings:
        for way in range(2):
            ring.arrived(way, XS // 2)
    c_copy(0, 0, False).wait_recv()
    for d in range(1, ys // 2 + 1):
        for way in range(2):
            c_copy(way, d, False).wait_recv()

    def r_copy(date, d, slot_at):
        return pltpu.make_async_remote_copy(
            src_ref=part.at[date, slot_at],
            dst_ref=back.at[date, d],
            send_sem=r_send.at[date, d],
            recv_sem=r_recv.at[date, d],
            device_id={"fac": lax.rem(z + d, zs) * XS + x},
            device_id_type=MESH,
        )

    tall = local * jn
    for date in range(DATES):
        total = None
        for at in range(XS):
            term = jnp.dot(
                pg[date, at],
                mg[:, at * tall : (at + 1) * tall, :].reshape(scen_n * tall, sets),
                preferred_element_type=F32,
            )
            total = term if total is None else total + term
        turned = total.T.reshape(zs, SETS, rows)
        nets[date] = turned
        part[date] = turned.astype(BF16)
        for d in range(1, zs):
            r_copy(date, d, lax.rem(z + d, zs)).start()
    for date in range(DATES):
        total = nets[date, z]
        for d in range(1, zs):
            r_copy(date, d, 0).wait_recv()
            total = total + back[date, d].astype(F32)
        expo[date] = jnp.maximum(total, 0.0)

    both = jnp.concatenate([expo[date] for date in range(DATES)], axis=0)
    ones = jnp.ones((8, rows), F32)
    row = lax.dot_general(
        ones, both, NT, precision=lax.Precision.HIGHEST, preferred_element_type=F32
    )
    sums[0] = row[0:1]

    def s_copy(d):
        return pltpu.make_async_remote_copy(
            src_ref=sums.at[0],
            dst_ref=sums.at[d],
            send_sem=s_send.at[d],
            recv_sem=s_recv.at[d],
            device_id={"scen": lax.rem(scen + d, scen_n)},
            device_id_type=MESH,
        )

    for d in range(1, scen_n):
        s_copy(d).start()
    for d in range(1, scen_n):
        s_copy(d).wait_recv()
    average = jnp.sum(sums[...], axis=0) / (rows * scen_n)
    for date in range(DATES):
        mean[date : date + 1, :] = average[:, date * SETS : (date + 1) * SETS]

    for kind in range(2):
        for d in range(1, zs):
            z_copy(kind, d, z).wait_send()
        for d in range(1, XS):
            x_copy(kind, d, x).wait_send()
    for ring in p_rings:
        ring.sent()
    m_ring.sent()
    c_copy(0, 0, True).wait_send()
    for d in range(1, ys // 2 + 1):
        for way in range(2):
            c_copy(way, d, True).wait_send()
    for date in range(DATES):
        for d in range(1, zs):
            r_copy(date, d, 0).wait_send()
    for d in range(1, scen_n):
        s_copy(d).wait_send()


def body(
    shocks,
    loadings,
    vol,
    jump_counts,
    jump_noise,
    jump_mean,
    jump_vol,
    dependencies,
    block_slot,
    trade_weights,
    netting,
):
    fac_n = lax.axis_size("fac")
    scen_n = lax.axis_size("scen")
    zs = fac_n // XS
    ys = scen_n // CORES
    rows = shocks.shape[1]
    width = loadings.shape[1]
    trades = netting.shape[0]
    local = width // BLOCK
    jn = BLOCK // scen_n
    tall = XS * local * jn
    sets = zs * SETS
    vmem = pl.BlockSpec(memory_space=pltpu.VMEM)
    smem = pl.BlockSpec(memory_space=pltpu.SMEM)
    dma = pltpu.SemaphoreType.DMA
    return pl.pallas_call(
        functools.partial(kernel, fac_n, scen_n),
        out_shape=(
            jax.ShapeDtypeStruct((DATES, SETS, rows), F32),
            jax.ShapeDtypeStruct((DATES, SETS), F32),
        ),
        in_specs=[vmem] * 8 + [smem] + [vmem] * 2,
        out_specs=(vmem, vmem),
        scratch_shapes=[
            pltpu.VMEM((2 * trades, BLOCK), F32),
            pltpu.VMEM((XS, zs, 1, 3 * trades), jnp.int32),
            pltpu.VMEM((XS, zs, 2 * jn, trades), BF16),
            pltpu.VMEM((sets, zs * trades), BF16),
            pltpu.VMEM((tall, zs * trades), BF16),
            pltpu.VMEM((tall, sets), F32),
            pltpu.VMEM((scen_n, tall, sets), BF16),
            pltpu.VMEM((rows, width), F32),
            pltpu.VMEM((DATES, XS, rows, width), BF16),
            pltpu.VMEM((DATES, zs, SETS, rows), F32),
            pltpu.VMEM((DATES, zs, SETS, rows), BF16),
            pltpu.VMEM((DATES, zs, SETS, rows), BF16),
            pltpu.VMEM((scen_n, 1, DATES * SETS), F32),
            dma((2, zs)),
            dma((2, zs)),
            dma((2, XS)),
            dma((2, XS)),
            dma((DATES, 2, XS // 2 + 1)),
            dma((DATES, 2, XS // 2 + 1)),
            dma((2, ys // 2 + 1)),
            dma((2, ys // 2 + 1)),
            dma((2, ys // 2 + 1)),
            dma((2, ys // 2 + 1)),
            dma((DATES, zs)),
            dma((DATES, zs)),
            dma((scen_n,)),
            dma((scen_n,)),
        ],
        compiler_params=pltpu.CompilerParams(
            collective_id=0, has_side_effects=True, vmem_limit_bytes=48 * 1024 * 1024
        ),
    )(
        shocks,
        loadings,
        vol.reshape(1, width),
        jump_counts,
        jump_noise,
        jump_mean.reshape(1, width),
        jump_vol.reshape(1, width),
        dependencies.T,
        block_slot,
        trade_weights.reshape(2 * trades, BLOCK),
        netting.reshape(1, trades),
    )


def solution(mesh):
    placed = (
        P(None, "scen", None),
        P(None, "fac"),
        P("fac"),
        P(None, "scen", "fac"),
        P(None, "scen", "fac"),
        P("fac"),
        P("fac"),
        P("fac", None),
        P(),
        P("fac", None, None),
        P("fac"),
    )
    return jax.shard_map(
        body,
        mesh=mesh,
        in_specs=placed,
        out_specs=(P(None, "fac", "scen"), P(None, "fac")),
        check_vma=False,
    )
```

time: 684 us -> 73.7 us (0.11)
  waiting for transfers between devices: 605 us -> 0 us
  Pallas kernels: 0 us -> 66.1 us
  blocking collectives: 28.8 us -> 0 us
  matrix products: 21 us -> 0 us
  between operations: 13.9 us -> 0.7 us
  other arithmetic: 11.6 us -> 0 us
    reduce_scatter x2 -> x0, waiting for transfers between devices: 439 us -> none  [body(): lax.psum_scatter(partial_value, 'fac', scatter_dimension=0, tiled=True)]
    all_gather x2 -> x0, waiting for transfers between devices: 165 us -> none  [body(): lax.all_gather(prices, 'fac', axis=1, tiled=True)]
    pallas_call x0 -> x1, Pallas kernels: none -> 66.1 us  [body(): pl.pallas_call(functools.partial(kernel, fac_n, scen_n), out_shape=(jax.S...]
    psum x1 -> x0, blocking collectives: 28.8 us -> none  [body(): summed = lax.psum(jnp.stack(totals), 'scen')]
    dot_general x5 -> x0, matrix products: 21 us -> none  [the longest x2 12.6 us: body(): jnp.dot(lax.all_gather(prices, 'fac', axis=1, tiled=True), dense, preferr...]
    scatter-add x2 -> x0, other arithmetic: 7.07 us -> none  [body(): jax.ops.segment_sum(values.T, netting, num_segments=set_total)]
  transfers between devices with their start and end apart: 4 -> 0, of which waited for: 4 -> 0; matrix products, arithmetic and copies ran while one was open for 4% -> 0% of each run, Pallas kernels for 0% -> 0%
where the time goes in v1:
time: 73.7 us; the launch traced here: 73.5 us
  Pallas kernels  66.1 us (90%)
  local copies, waits for them, and re-layouts  6.66 us (9%)
    pallas_call x1, Pallas kernels, body(): pl.pallas_call(functools.partial(kernel, fac_n, scen_n), out_shape=(jax.S...  66.1 us
    unnamed x24, local copies, waits for them, and re-layouts  6.66 us

profile of v1, /device:TPU:1, one launch (start us, length us, event | category | flops | bytes accessed | tf_op | source)
XLA Modules:
  0.0 73.5 jit_solution(2936856638722816893)
XLA Ops:
  0.6 0.0 copy-start.9
  0.6 0.0 copy-start.7
  0.7 0.0 copy-start.8
  0.7 0.0 copy-start.5
  0.7 0.0 copy-start.6
  0.7 0.0 copy-start.10
  0.7 0.6 copy-done.9
  1.3 0.0 copy-done.7
  1.3 0.0 copy-done.8
  1.3 0.0 copy-done.5
  1.4 0.0 copy-done.6
  1.4 0.0 copy-done.10
  1.4 0.0 copy-start
  1.4 1.0 %copy-done = s32[2,256,256]{2,1,0:T(8,128)S(1)} copy-done((s32[2,256,256]{2,1,0:T(8,128)S(1)}, s32[2,256,256]{2,1,0:T(8,128)}, u32[]{:S(2)}) %copy-start) | copy-done | bytes 524312
  2.4 0.0 copy-start.1
  2.4 0.9 %copy-done.1 = bf16[2,256,256]{2,1,0:T(8,128)(2,1)S(1)} copy-done((bf16[2,256,256]{2,1,0:T(8,128)(2,1)S(1)}, bf16[2,256,256]{2,1,0:T(8,128)(2,1)}, u32[]{:S(2)}) %copy-start.1) | copy-done | bytes 262168
  3.4 0.0 copy-start.2
  3.4 0.9 %copy-done.2 = bf16[2,256,256]{2,1,0:T(8,128)(2,1)S(1)} copy-done((bf16[2,256,256]{2,1,0:T(8,128)(2,1)S(1)}, bf16[2,256,256]{2,1,0:T(8,128)(2,1)}, u32[]{:S(2)}) %copy-start.2) | copy-done | bytes 262168
  4.3 0.0 copy-start.3
  4.3 0.9 %copy-done.3 = bf16[256,256]{1,0:T(8,128)(2,1)S(1)} copy-done((bf16[256,256]{1,0:T(8,128)(2,1)S(1)}, bf16[256,256]{1,0:T(8,128)(2,1)}, u32[]{:S(2)}) %copy-start.3) | copy-done | bytes 131096
  5.2 0.9 %copy-done.4 = bf16[256,2,128]{2,1,0:T(2,128)(2,1)S(1)} copy-done((bf16[256,2,128]{2,1,0:T(2,128)(2,1)S(1)}, bf16[256,2,128]{2,1,0:T(2,128)(2,1)}, u32[]{:S(2)}) %copy-start.4) | copy-done | bytes 131096
  6.1 66.1 %shard_map.122 = (f32[2,64,256]{2,1,0:T(8,128)S(1)}, f32[2,64]{1,0:T(2,128)S(1)}) custom-call(bf16[2,256,256]{2,1,0:T(8,128)(2,1)S(1)} %copy-done.1, bf16[256,256]{1,0:T(8,128)(2,1)S(1)} %copy-done.3, f32[1,256]{1,0:T(1,128)S(1)} %bitcast.8, s32[2,256,256]{2,1,0:T(8,128)S(1)} %copy-done, bf16[2,256,256]{2,1,0:T(8,128)(2,1)S(1)} %copy-done.2, ...), custom_call_target="tpu_custom_call" | custom-call | tf_op jit(solution)/shard_map/pallas_call | solution.py:422
  72.2 0.7 copy.15
  72.9 0.6 copy.16
  (1 shorter events, 0.0 us)
Async XLA Ops:
  0.6 0.7 copy-start.9
  0.6 0.7 copy-start.7
  0.7 0.7 copy-start.8
  0.7 0.7 copy-start.5
  0.7 0.7 copy-start.6
  0.7 0.7 copy-start.10
  1.4 1.0 %copy-start = (s32[2,256,256]{2,1,0:T(8,128)S(1)}, s32[2,256,256]{2,1,0:T(8,128)}, u32[]{:S(2)}) copy-start(s32[2,256,256]{2,1,0:T(8,128)} %counts.1) | copy-start | bytes 1572868
  2.4 0.9 %copy-start.1 = (bf16[2,256,256]{2,1,0:T(8,128)(2,1)S(1)}, bf16[2,256,256]{2,1,0:T(8,128)(2,1)}, u32[]{:S(2)}) copy-start(bf16[2,256,256]{2,1,0:T(8,128)(2,1)} %shocks.1) | copy-start | bytes 786436
  3.4 0.9 %copy-start.2 = (bf16[2,256,256]{2,1,0:T(8,128)(2,1)S(1)}, bf16[2,256,256]{2,1,0:T(8,128)(2,1)}, u32[]{:S(2)}) copy-start(bf16[2,256,256]{2,1,0:T(8,128)(2,1)} %noise.1) | copy-start | bytes 786436
  4.3 0.9 %copy-start.3 = (bf16[256,256]{1,0:T(8,128)(2,1)S(1)}, bf16[256,256]{1,0:T(8,128)(2,1)}, u32[]{:S(2)}) copy-start(bf16[256,256]{1,0:T(8,128)(2,1)} %loadings.1) | copy-start | bytes 393220
  5.2 0.9 %copy-start.4 = (bf16[256,2,128]{2,1,0:T(2,128)(2,1)S(1)}, bf16[256,2,128]{2,1,0:T(2,128)(2,1)}, u32[]{:S(2)}) copy-start(bf16[256,2,128]{2,1,0:T(2,128)(2,1)} %param.20) | copy-start | bytes 393220

commit v2 on v1

v2 whole, which is shorter than its diff:
```python
import functools

import jax
import jax.numpy as jnp
from jax import lax
from jax.experimental import pallas as pl
from jax.experimental.pallas import tpu as pltpu
from jax.sharding import PartitionSpec as P

BLOCK = 128
SETS = 64
DATES = 2
CORES = 2
XS = 4
P_CUTS = 2
M_CUTS = 2
MESH = pl.DeviceIdType.MESH
F32 = jnp.float32
BF16 = jnp.bfloat16
NT = (((1,), (1,)), ((), ()))
INPUTS = 11
FIRST = (8, 7, 10, 9)
LATER = (0, 1, 3, 4, 2, 5, 6)


class Ring:
    def __init__(self, n, me, axis, device, view, send, recv, cuts):
        self.n, self.me, self.axis, self.device, self.view = n, me, axis, device, view
        self.send, self.recv, self.cuts = send, recv, cuts
        self.last = n // 2

    def pieces(self, way, d):
        half = self.cuts // 2
        if d < self.last:
            return range(self.cuts)
        return range(way * half, (way + 1) * half)

    def owner(self, way, d):
        step = -d if way == 0 else d
        return lax.rem(self.me + step + self.n, self.n)

    def copy(self, way, d, piece, shift):
        ref = self.view(self.owner(way, d - shift), piece)
        to = self.owner(way, -1)
        return pltpu.make_async_remote_copy(
            src_ref=ref,
            dst_ref=ref,
            send_sem=self.send.at[way, d, piece],
            recv_sem=self.recv.at[way, d, piece],
            device_id={self.axis: self.device(to)},
            device_id_type=MESH,
        )

    def begin(self):
        for piece in range(self.cuts):
            for way in range(2):
                if piece in self.pieces(way, 1):
                    self.copy(way, 1, piece, 1).start()

    def step(self, d, also=None):
        for piece in range(self.cuts):
            for way in range(2):
                if piece in self.pieces(way, d):
                    self.copy(way, d, piece, 0).wait_recv()
                    if d < self.last and piece in self.pieces(way, d + 1):
                        self.copy(way, d + 1, piece, 1).start()
                    if also is not None:
                        also(way, d, piece)

    def sent(self):
        for d in range(1, self.last + 1):
            for way in range(2):
                for piece in self.pieces(way, d):
                    self.copy(way, d, piece, 1).wait_send()


def kernel(
    fac_n,
    scen_n,
    *refs,
):
    given, refs = refs[:INPUTS], refs[INPUTS:]
    expo, mean, *refs = refs
    held, refs = refs[:INPUTS], refs[INPUTS:]
    run(fac_n, scen_n, given, held, expo, mean, *refs)


def run(
    fac_n,
    scen_n,
    given,
    held,
    expo,
    mean,
    load_sem,
    w32,
    keys,
    wg,
    marks,
    spread,
    macc,
    mg,
    level,
    pg,
    nets,
    part,
    back,
    sums,
    z_send,
    z_recv,
    x_send,
    x_recv,
    p_send,
    p_recv,
    m_send,
    m_recv,
    c_send,
    c_recv,
    r_send,
    r_recv,
    s_send,
    s_recv,
):
    loads = [
        pltpu.make_async_copy(src, dst, load_sem.at[i])
        for i, (src, dst) in enumerate(zip(given, held))
    ]
    for i in FIRST:
        loads[i].start()
    for i in LATER:
        loads[i].start()
    (shocks, loadings, vol, counts, noise, jump_mean, jump_vol, deps, place, weights, netting) = (
        held
    )
    zs = fac_n // XS
    ys = scen_n // CORES
    rows = shocks.shape[1]
    width = loadings.shape[1]
    local = width // BLOCK
    trades = netting.shape[1]
    jn = BLOCK // scen_n
    fac = lax.axis_index("fac")
    scen = lax.axis_index("scen")
    z, x = fac // XS, lax.rem(fac, XS)
    y, c = scen // CORES, lax.rem(scen, CORES)

    barrier = pltpu.get_barrier_semaphore()
    partners = 0
    for d in range(1, zs):
        pl.semaphore_signal(
            barrier, inc=1, device_id={"fac": lax.rem(z + d, zs) * XS + x}, device_id_type=MESH
        )
        partners += 1
    for d in range(1, XS):
        pl.semaphore_signal(
            barrier, inc=1, device_id={"fac": z * XS + lax.rem(x + d, XS)}, device_id_type=MESH
        )
        partners += 1
    for d in range(1, scen_n):
        pl.semaphore_signal(
            barrier, inc=1, device_id={"scen": lax.rem(scen + d, scen_n)}, device_id_type=MESH
        )
        partners += 1

    for i in FIRST:
        loads[i].wait()

    dep = deps[...]
    slot = jnp.zeros_like(dep)
    for b in range(place.shape[0]):
        slot = jnp.where(dep == b, place[b], slot)
    keys[x, z, :, 0:trades] = slot[0:1]
    keys[x, z, :, trades : 2 * trades] = slot[1:2]
    keys[x, z, :, 2 * trades : 3 * trades] = netting[...]
    w32[...] = weights[...].astype(F32)
    pick = (
        lax.broadcasted_iota(jnp.int32, (jn, BLOCK), 1)
        == lax.broadcasted_iota(jnp.int32, (jn, BLOCK), 0) + scen * jn
    ).astype(F32).astype(BF16)
    chosen = [
        lax.dot_general(
            pick, w32[pl.ds(k, trades, stride=2), :].astype(BF16), NT, preferred_element_type=F32
        )
        for k in range(2)
    ]
    wg[x, z] = jnp.concatenate(chosen, axis=0).astype(BF16)

    def z_copy(kind, d, from_z):
        ref = keys.at[x, from_z] if kind == 0 else wg.at[x, from_z]
        return pltpu.make_async_remote_copy(
            src_ref=ref,
            dst_ref=ref,
            send_sem=z_send.at[kind, d],
            recv_sem=z_recv.at[kind, d],
            device_id={"fac": lax.rem(z + d, zs) * XS + x},
            device_id_type=MESH,
        )

    def x_copy(kind, d, from_x):
        ref = keys.at[from_x] if kind == 0 else wg.at[from_x]
        return pltpu.make_async_remote_copy(
            src_ref=ref,
            dst_ref=ref,
            send_sem=x_send.at[kind, d],
            recv_sem=x_recv.at[kind, d],
            device_id={"fac": z * XS + lax.rem(x + d, XS)},
            device_id_type=MESH,
        )

    pl.semaphore_wait(barrier, partners)
    for kind in range(2):
        for d in range(1, zs):
            z_copy(kind, d, z).start()
    for i in LATER:
        loads[i].wait()

    p_rings = []
    cut_rows = rows // P_CUTS
    for date in range(DATES):

        def p_view(owner, piece, date=date):
            return pg.at[date, owner, pl.ds(piece * cut_rows, cut_rows)]

        p_rings.append(
            Ring(
                zs,
                z,
                "fac",
                lambda i: i * XS + x,
                p_view,
                p_send.at[date],
                p_recv.at[date],
                P_CUTS,
            )
        )

    col_q = lax.broadcasted_iota(jnp.int32, (width, width), 1)
    col_f = (
        lax.rem(lax.div(col_q, jn), local) * BLOCK
        + lax.div(col_q, jn * local) * jn
        + lax.rem(col_q, jn)
    )
    perm = (lax.broadcasted_iota(jnp.int32, (width, width), 0) == col_f).astype(F32).astype(BF16)
    v = vol[...]
    drift = 0.5 * v * v
    for date in range(DATES):
        diffuse = jnp.dot(shocks[date], loadings[...], preferred_element_type=F32)
        number = counts[date].astype(F32)
        change = (
            v * diffuse
            - drift
            + number * jump_mean[...]
            + jnp.sqrt(number) * jump_vol[...] * noise[date].astype(F32)
        )
        now = change if date == 0 else level[...] + change
        if date < DATES - 1:
            level[...] = now
        prices = (jnp.exp(now) - 1.0).astype(BF16)
        pg[date, z] = jnp.dot(prices, perm, preferred_element_type=F32).astype(BF16)

    for kind in range(2):
        for d in range(1, zs):
            z_copy(kind, d, lax.rem(z - d + zs, zs)).wait_recv()
    for kind in range(2):
        for d in (1, XS - 1, 2):
            x_copy(kind, d, x).start()
    for ring in p_rings:
        ring.begin()
    sets = XS * SETS
    macc[...] = jnp.zeros_like(macc)

    def form(owner):
        @pl.loop(0, zs)
        def _(at):
            columns = pl.ds(pl.multiple_of(at * trades, trades), trades)
            key = keys[owner, at]
            line = key[:, 2 * trades : 3 * trades] - sets * z
            marks[:, columns] = jnp.where(
                lax.broadcasted_iota(jnp.int32, (sets, trades), 0) == line, 1.0, 0.0
            ).astype(BF16)
            w = wg[owner, at].astype(F32)
            w0, w1 = w[0:jn], w[jn : 2 * jn]
            first = key[:, 0:trades] - local * x
            second = key[:, trades : 2 * trades] - local * x
            spread[:, columns] = jnp.concatenate(
                [
                    jnp.where(first == b, w0, 0.0) + jnp.where(second == b, w1, 0.0)
                    for b in [
                        to_z * XS * local + of for to_z in range(zs) for of in range(local)
                    ]
                ],
                axis=0,
            ).astype(BF16)

        macc[...] += lax.dot_general(spread[...], marks[...], NT, preferred_element_type=F32)

    form(x)
    for d in (1, XS - 1, 2):
        from_x = lax.rem(x - d + XS, XS)
        for kind in range(2):
            x_copy(kind, d, from_x).wait_recv()
        form(from_x)
    mg[scen] = macc[...].astype(BF16)

    cut_tall = macc.shape[0] // M_CUTS

    def m_view(core):
        def view(owner, piece):
            return mg.at[owner * CORES + core, pl.ds(piece * cut_tall, cut_tall)]

        return view

    m_ring = Ring(ys, y, "scen", lambda i: i * CORES + c, m_view(c), m_send, m_recv, M_CUTS)
    other = 1 - c

    def c_copy(way, d, piece, core):
        ref = m_view(core)(m_ring.owner(way, d), piece)
        return pltpu.make_async_remote_copy(
            src_ref=ref,
            dst_ref=ref,
            send_sem=c_send.at[way, d, piece],
            recv_sem=c_recv.at[way, d, piece],
            device_id={"scen": y * CORES + other},
            device_id_type=MESH,
        )

    def pass_on(way, d, piece):
        c_copy(way, d, piece, c).start()

    c_pieces = [(0, 0, piece) for piece in range(M_CUTS)] + [
        (way, d, piece)
        for d in range(1, ys // 2 + 1)
        for way in range(2)
        for piece in m_ring.pieces(way, d)
    ]
    m_ring.begin()
    for piece in range(M_CUTS):
        pass_on(0, 0, piece)
    for d in range(1, max(ys, zs) // 2 + 1):
        if d <= zs // 2:
            for ring in p_rings:
                ring.step(d)
        if d <= ys // 2:
            m_ring.step(d, pass_on)
    for way, d, piece in c_pieces:
        c_copy(way, d, piece, other).wait_recv()

    def r_copy(date, d, slot_at):
        return pltpu.make_async_remote_copy(
            src_ref=part.at[date, slot_at],
            dst_ref=back.at[date, d],
            send_sem=r_send.at[date, d],
            recv_sem=r_recv.at[date, d],
            device_id={"fac": z * XS + lax.rem(x + d, XS)},
            device_id_type=MESH,
        )

    tall = local * jn
    for date in range(DATES):
        total = None
        for at in range(zs):
            term = jnp.dot(
                pg[date, at],
                mg[:, at * tall : (at + 1) * tall, :].reshape(scen_n * tall, sets),
                preferred_element_type=F32,
            )
            total = term if total is None else total + term
        turned = total.T.reshape(XS, SETS, rows)
        nets[date] = turned
        part[date] = turned.astype(BF16)
        for d in (1, XS - 1, 2):
            r_copy(date, d, lax.rem(x + d, XS)).start()
    for date in range(DATES):
        total = nets[date, x]
        for d in (1, XS - 1, 2):
            r_copy(date, d, 0).wait_recv()
            total = total + back[date, d].astype(F32)
        expo[date] = jnp.maximum(total, 0.0)

    both = jnp.concatenate([expo[date] for date in range(DATES)], axis=0)
    ones = jnp.ones((8, rows), F32)
    row = lax.dot_general(
        ones, both, NT, precision=lax.Precision.HIGHEST, preferred_element_type=F32
    )
    sums[0] = row[0:1]

    def s_copy(d):
        return pltpu.make_async_remote_copy(
            src_ref=sums.at[0],
            dst_ref=sums.at[d],
            send_sem=s_send.at[d],
            recv_sem=s_recv.at[d],
            device_id={"scen": lax.rem(scen + d, scen_n)},
            device_id_type=MESH,
        )

    for d in range(1, scen_n):
        s_copy(d).start()
    for d in range(1, scen_n):
        s_copy(d).wait_recv()
    average = jnp.sum(sums[...], axis=0) / (rows * scen_n)
    for date in range(DATES):
        mean[date : date + 1, :] = average[:, date * SETS : (date + 1) * SETS]

    for kind in range(2):
        for d in range(1, zs):
            z_copy(kind, d, z).wait_send()
        for d in range(1, XS):
            x_copy(kind, d, x).wait_send()
    for ring in p_rings:
        ring.sent()
    m_ring.sent()
    for way, d, piece in c_pieces:
        c_copy(way, d, piece, c).wait_send()
    for date in range(DATES):
        for d in range(1, XS):
            r_copy(date, d, 0).wait_send()
    for d in range(1, scen_n):
        s_copy(d).wait_send()


def body(
    shocks,
    loadings,
    vol,
    jump_counts,
    jump_noise,
    jump_mean,
    jump_vol,
    dependencies,
    block_slot,
    trade_weights,
    netting,
):
    fac_n = lax.axis_size("fac")
    scen_n = lax.axis_size("scen")
    zs = fac_n // XS
    ys = scen_n // CORES
    rows = shocks.shape[1]
    width = loadings.shape[1]
    trades = netting.shape[0]
    local = width // BLOCK
    jn = BLOCK // scen_n
    tall = zs * local * jn
    sets = XS * SETS
    vmem = pl.BlockSpec(memory_space=pltpu.VMEM)
    hbm = pl.BlockSpec(memory_space=pltpu.HBM)
    dma = pltpu.SemaphoreType.DMA
    arrays = (
        shocks,
        loadings,
        vol.reshape(1, width),
        jump_counts,
        jump_noise,
        jump_mean.reshape(1, width),
        jump_vol.reshape(1, width),
        dependencies.T,
        block_slot,
        trade_weights.reshape(2 * trades, BLOCK),
        netting.reshape(1, trades),
    )
    return pl.pallas_call(
        functools.partial(kernel, fac_n, scen_n),
        out_shape=(
            jax.ShapeDtypeStruct((DATES, SETS, rows), F32),
            jax.ShapeDtypeStruct((DATES, SETS), F32),
        ),
        in_specs=[hbm] * INPUTS,
        out_specs=(vmem, vmem),
        scratch_shapes=[
            (pltpu.SMEM if i == 8 else pltpu.VMEM)(a.shape, a.dtype) for i, a in enumerate(arrays)
        ]
        + [
            dma((INPUTS,)),
            pltpu.VMEM((2 * trades, BLOCK), F32),
            pltpu.VMEM((XS, zs, 1, 3 * trades), jnp.int32),
            pltpu.VMEM((XS, zs, 2 * jn, trades), BF16),
            pltpu.VMEM((sets, zs * trades), BF16),
            pltpu.VMEM((tall, zs * trades), BF16),
            pltpu.VMEM((tall, sets), F32),
            pltpu.VMEM((scen_n, tall, sets), BF16),
            pltpu.VMEM((rows, width), F32),
            pltpu.VMEM((DATES, zs, rows, width), BF16),
            pltpu.VMEM((DATES, XS, SETS, rows), F32),
            pltpu.VMEM((DATES, XS, SETS, rows), BF16),
            pltpu.VMEM((DATES, XS, SETS, rows), BF16),
            pltpu.VMEM((scen_n, 1, DATES * SETS), F32),
            dma((2, zs)),
            dma((2, zs)),
            dma((2, XS)),
            dma((2, XS)),
            dma((DATES, 2, zs // 2 + 1, P_CUTS)),
            dma((DATES, 2, zs // 2 + 1, P_CUTS)),
            dma((2, ys // 2 + 1, M_CUTS)),
            dma((2, ys // 2 + 1, M_CUTS)),
            dma((2, ys // 2 + 1, M_CUTS)),
            dma((2, ys // 2 + 1, M_CUTS)),
            dma((DATES, XS)),
            dma((DATES, XS)),
            dma((scen_n,)),
            dma((scen_n,)),
        ],
        compiler_params=pltpu.CompilerParams(
            collective_id=0, has_side_effects=True, vmem_limit_bytes=60 * 1024 * 1024
        ),
    )(*arrays)


def solution(mesh):
    placed = (
        P(None, "scen", None),
        P(None, "fac"),
        P("fac"),
        P(None, "scen", "fac"),
        P(None, "scen", "fac"),
        P("fac"),
        P("fac"),
        P("fac", None),
        P(),
        P("fac", None, None),
        P("fac"),
    )
    return jax.shard_map(
        body,
        mesh=mesh,
        in_specs=placed,
        out_specs=(P(None, "fac", "scen"), P(None, "fac")),
        check_vma=False,
    )
```

time: 73.7 us -> 62.4 us (0.85)
  Pallas kernels: 66.1 us -> 59.4 us
  local copies, waits for them, and re-layouts: 6.66 us -> 2.13 us
    pallas_call x1, Pallas kernels: 66.1 us -> 59.4 us  [body(): pl.pallas_call(functools.partial(kernel, fac_n, scen_n), out_shape=(jax.S...]
    unnamed x24 -> x4, local copies, waits for them, and re-layouts: 6.66 us -> 2.13 us
where the time goes in v2:
time: 62.4 us; the launch traced here: 62.2 us
  Pallas kernels  59.4 us (95%)
  local copies, waits for them, and re-layouts  2.13 us (3%)
  between operations  0.65 us (1%)
    pallas_call x1, Pallas kernels, body(): pl.pallas_call(functools.partial(kernel, fac_n, scen_n), out_shape=(jax.S...  59.4 us
    unnamed x4, local copies, waits for them, and re-layouts  2.13 us

profile of v2, /device:TPU:1, one launch (start us, length us, event | category | flops | bytes accessed | tf_op | source)
XLA Modules:
  0.0 62.2 jit_solution(37240289450423793)
XLA Ops:
  0.6 59.4 %shard_map.122 = (f32[2,64,256]{2,1,0:T(8,128)}, f32[2,64]{1,0:T(2,128)}) custom-call(bf16[2,256,256]{2,1,0:T(8,128)(2,1)} %refs_0_.1, bf16[256,256]{1,0:T(8,128)(2,1)} %refs_1_.1, f32[1,256]{1,0:T(1,128)} %bitcast.8, s32[2,256,256]{2,1,0:T(8,128)} %refs_3_.1, bf16[2,256,256]{2,1,0:T(8,128)(2,1)} %refs_4_.1, f32[1,256]{1,0:T(1,128)} %bitcast.9, ...), custom_call_target="tpu_custom_call" | custom-call | tf_op jit(solution)/shard_map/pallas_call | solution.py:462
  60.1 0.0 copy-start
  60.1 1.6 %copy.15 = f32[2,64,256]{2,1,0:T(8,128)} copy(f32[2,64,256]{2,1,0:T(8,128)} %get-tuple-element.4) | data formatting | bytes 262144
  61.7 0.0 copy-done
  61.7 0.6 copy.16
Async XLA Ops:
  60.1 1.6 %copy-start = (f32[2,64]{1,0:T(2,128)S(1)}, f32[2,64]{1,0:T(2,128)}, u32[]{:S(2)}) copy-start(f32[2,64]{1,0:T(2,128)} %get-tuple-element.5) | copy-start | bytes 1540

commit v3 on v2

--- a/solution.py
+++ b/solution.py
@@ -24,9 +24,9 @@
 
 
 class Ring:
-    def __init__(self, n, me, axis, device, view, send, recv, cuts):
+    def __init__(self, n, me, axis, device, view, send, recv, cuts, hops):
         self.n, self.me, self.axis, self.device, self.view = n, me, axis, device, view
-        self.send, self.recv, self.cuts = send, recv, cuts
+        self.send, self.recv, self.cuts, self.hops = send, recv, cuts, hops
         self.last = n // 2
 
     def pieces(self, way, d):
@@ -41,7 +41,7 @@
 
     def copy(self, way, d, piece, shift):
         ref = self.view(self.owner(way, d - shift), piece)
-        to = self.owner(way, -1)
+        to = self.owner(way, -self.hops[d])
         return pltpu.make_async_remote_copy(
             src_ref=ref,
             dst_ref=ref,
@@ -51,19 +51,26 @@
             device_id_type=MESH,
         )
 
+    def start(self, way, d, piece):
+        self.copy(way, d, piece, self.hops[d]).start()
+
     def begin(self):
-        for piece in range(self.cuts):
-            for way in range(2):
-                if piece in self.pieces(way, 1):
-                    self.copy(way, 1, piece, 1).start()
+        for d in range(self.last, 0, -1):
+            for piece in range(self.cuts):
+                for way in range(2):
+                    if d == self.hops[d] and piece in self.pieces(way, d):
+                        self.start(way, d, piece)
 
     def step(self, d, also=None):
+        if d > self.last:
+            return
         for piece in range(self.cuts):
             for way in range(2):
                 if piece in self.pieces(way, d):
                     self.copy(way, d, piece, 0).wait_recv()
-                    if d < self.last and piece in self.pieces(way, d + 1):
-                        self.copy(way, d + 1, piece, 1).start()
+                    for later in range(d + 1, self.last + 1):
+                        if later - self.hops[later] == d and piece in self.pieces(way, later):
+                            self.start(way, later, piece)
                     if also is not None:
                         also(way, d, piece)
 
@@ -71,7 +78,7 @@
         for d in range(1, self.last + 1):
             for way in range(2):
                 for piece in self.pieces(way, d):
-                    self.copy(way, d, piece, 1).wait_send()
+                    self.copy(way, d, piece, self.hops[d]).wait_send()
 
 
 def kernel(
@@ -169,9 +176,9 @@
     slot = jnp.zeros_like(dep)
     for b in range(place.shape[0]):
         slot = jnp.where(dep == b, place[b], slot)
-    keys[x, z, :, 0:trades] = slot[0:1]
-    keys[x, z, :, trades : 2 * trades] = slot[1:2]
-    keys[x, z, :, 2 * trades : 3 * trades] = netting[...]
+    keys[x, 0, :, 0:trades] = slot[0:1]
+    keys[x, 0, :, trades : 2 * trades] = slot[1:2]
+    keys[x, 0, :, 2 * trades : 3 * trades] = netting[...]
     w32[...] = weights[...].astype(F32)
     pick = (
         lax.broadcasted_iota(jnp.int32, (jn, BLOCK), 1)
@@ -183,34 +190,42 @@
         )
         for k in range(2)
     ]
-    wg[x, z] = jnp.concatenate(chosen, axis=0).astype(BF16)
-
-    def z_copy(kind, d, from_z):
-        ref = keys.at[x, from_z] if kind == 0 else wg.at[x, from_z]
+    wg[x, 0] = jnp.concatenate(chosen, axis=0).astype(BF16)
+
+    near = [0]
+    for d in range(1, zs // 2 + 1):
+        near += [d] if 2 * d == zs else [d, zs - d]
+    cut = zs * 5 // 8
+    groups = ((0, cut), (cut, zs))
+
+    def z_copy(kind, d):
+        buffer = keys if kind == 0 else wg
         return pltpu.make_async_remote_copy(
-            src_ref=ref,
-            dst_ref=ref,
+            src_ref=buffer.at[x, 0],
+            dst_ref=buffer.at[x, near.index(d)],
             send_sem=z_send.at[kind, d],
             recv_sem=z_recv.at[kind, d],
             device_id={"fac": lax.rem(z + d, zs) * XS + x},
             device_id_type=MESH,
         )
 
-    def x_copy(kind, d, from_x):
-        ref = keys.at[from_x] if kind == 0 else wg.at[from_x]
+    def x_copy(kind, d, piece, from_x):
+        buffer = keys if kind == 0 else wg
+        low, high = groups[piece]
+        ref = buffer.at[from_x, pl.ds(low, high - low)]
         return pltpu.make_async_remote_copy(
             src_ref=ref,
             dst_ref=ref,
-            send_sem=x_send.at[kind, d],
-            recv_sem=x_recv.at[kind, d],
+            send_sem=x_send.at[kind, d, piece],
+            recv_sem=x_recv.at[kind, d, piece],
             device_id={"fac": z * XS + lax.rem(x + d, XS)},
             device_id_type=MESH,
         )
 
     pl.semaphore_wait(barrier, partners)
-    for kind in range(2):
-        for d in range(1, zs):
-            z_copy(kind, d, z).start()
+    for d in near[:0:-1]:
+        for kind in range(2):
+            z_copy(kind, d).start()
     for i in LATER:
         loads[i].wait()
 
@@ -231,6 +246,7 @@
                 p_send.at[date],
                 p_recv.at[date],
                 P_CUTS,
+                (0, 1, 1, 1, 1),
             )
         )
 
@@ -257,15 +273,16 @@
             level[...] = now
         prices = (jnp.exp(now) - 1.0).astype(BF16)
         pg[date, z] = jnp.dot(prices, perm, preferred_element_type=F32).astype(BF16)
-
-    for kind in range(2):
-        for d in range(1, zs):
-            z_copy(kind, d, lax.rem(z - d + zs, zs)).wait_recv()
-    for kind in range(2):
-        for d in (1, XS - 1, 2):
-            x_copy(kind, d, x).start()
-    for ring in p_rings:
-        ring.begin()
+        p_rings[date].begin()
+
+    for piece, (low, high) in enumerate(groups):
+        for d in near[max(low, 1) : high]:
+            for kind in range(2):
+                z_copy(kind, d).wait_recv()
+        for d in (2, 1, XS - 1):
+            for kind in range(2):
+                x_copy(kind, d, piece, x).start()
+
     sets = XS * SETS
     macc[...] = jnp.zeros_like(macc)
 
@@ -294,12 +311,20 @@
 
         macc[...] += lax.dot_general(spread[...], marks[...], NT, preferred_element_type=F32)
 
+    def form_from(d):
+        from_x = lax.rem(x - d + XS, XS)
+        for piece in range(2):
+            for kind in range(2):
+                x_copy(kind, d, piece, from_x).wait_recv()
+        form(from_x)
+
     form(x)
-    for d in (1, XS - 1, 2):
-        from_x = lax.rem(x - d + XS, XS)
-        for kind in range(2):
-            x_copy(kind, d, from_x).wait_recv()
-        form(from_x)
+    for ring in p_rings:
+        ring.step(1)
+    form_from(1)
+    form_from(XS - 1)
+    p_rings[0].step(2)
+    form_from(2)
     mg[scen] = macc[...].astype(BF16)
 
     cut_tall = macc.shape[0] // M_CUTS
@@ -310,7 +335,17 @@
 
         return view
 
-    m_ring = Ring(ys, y, "scen", lambda i: i * CORES + c, m_view(c), m_send, m_recv, M_CUTS)
+    m_ring = Ring(
+        ys,
+        y,
+        "scen",
+        lambda i: i * CORES + c,
+        m_view(c),
+        m_send,
+        m_recv,
+        M_CUTS,
+        (0, 1, 2, 1, 2),
+    )
     other = 1 - c
 
     def c_copy(way, d, piece, core):
@@ -336,12 +371,15 @@
     m_ring.begin()
     for piece in range(M_CUTS):
         pass_on(0, 0, piece)
-    for d in range(1, max(ys, zs) // 2 + 1):
-        if d <= zs // 2:
-            for ring in p_rings:
-                ring.step(d)
-        if d <= ys // 2:
-            m_ring.step(d, pass_on)
+    p_rings[1].step(2)
+    p_rings[0].step(3)
+    m_ring.step(2, pass_on)
+    m_ring.step(1, pass_on)
+    p_rings[1].step(3)
+    m_ring.step(3, pass_on)
+    m_ring.step(4, pass_on)
+    for ring in p_rings:
+        ring.step(4)
     for way, d, piece in c_pieces:
         c_copy(way, d, piece, other).wait_recv()
 
@@ -404,9 +442,10 @@
 
     for kind in range(2):
         for d in range(1, zs):
-            z_copy(kind, d, z).wait_send()
+            z_copy(kind, d).wait_send()
         for d in range(1, XS):
-            x_copy(kind, d, x).wait_send()
+            for piece in range(2):
+                x_copy(kind, d, piece, x).wait_send()
     for ring in p_rings:
         ring.sent()
     m_ring.sent()
@@ -487,8 +526,8 @@
             pltpu.VMEM((scen_n, 1, DATES * SETS), F32),
             dma((2, zs)),
             dma((2, zs)),
-            dma((2, XS)),
-            dma((2, XS)),
+            dma((2, XS, 2)),
+            dma((2, XS, 2)),
             dma((DATES, 2, zs // 2 + 1, P_CUTS)),
             dma((DATES, 2, zs // 2 + 1, P_CUTS)),
             dma((2, ys // 2 + 1, M_CUTS)),

time: 62.4 us -> 58.5 us (0.938)
  Pallas kernels: 59.4 us -> 55.5 us
    pallas_call x1, Pallas kernels: 59.4 us -> 55.5 us  [body(): pl.pallas_call(functools.partial(kernel, fac_n, scen_n), out_shape=(jax.S...]
where the time goes in v3:
time: 58.5 us; the launch traced here: 58.3 us
  Pallas kernels  55.5 us (95%)
  local copies, waits for them, and re-layouts  2.13 us (4%)
  between operations  0.65 us (1%)
    pallas_call x1, Pallas kernels, body(): pl.pallas_call(functools.partial(kernel, fac_n, scen_n), out_shape=(jax.S...  55.5 us
    unnamed x4, local copies, waits for them, and re-layouts  2.13 us

profile of v3, /device:TPU:1, one launch (start us, length us, event | category | flops | bytes accessed | tf_op | source)
XLA Modules:
  0.0 58.3 jit_solution(13578599875144953538)
XLA Ops:
  0.6 55.5 %shard_map.122 = (f32[2,64,256]{2,1,0:T(8,128)}, f32[2,64]{1,0:T(2,128)}) custom-call(bf16[2,256,256]{2,1,0:T(8,128)(2,1)} %refs_0_.1, bf16[256,256]{1,0:T(8,128)(2,1)} %refs_1_.1, f32[1,256]{1,0:T(1,128)} %bitcast.8, s32[2,256,256]{2,1,0:T(8,128)} %refs_3_.1, bf16[2,256,256]{2,1,0:T(8,128)(2,1)} %refs_4_.1, f32[1,256]{1,0:T(1,128)} %bitcast.9, ...), custom_call_target="tpu_custom_call" | custom-call | tf_op jit(solution)/shard_map/pallas_call | solution.py:501
  56.2 0.0 copy-start
  56.2 1.6 %copy.15 = f32[2,64,256]{2,1,0:T(8,128)} copy(f32[2,64,256]{2,1,0:T(8,128)} %get-tuple-element.4) | data formatting | bytes 262144
  57.8 0.0 copy-done
  57.8 0.6 copy.16
Async XLA Ops:
  56.2 1.6 %copy-start = (f32[2,64]{1,0:T(2,128)S(1)}, f32[2,64]{1,0:T(2,128)}, u32[]{:S(2)}) copy-start(f32[2,64]{1,0:T(2,128)} %get-tuple-element.5) | copy-start | bytes 1540

commit v4 on v3

--- a/solution.py
+++ b/solution.py
@@ -275,19 +275,13 @@
         pg[date, z] = jnp.dot(prices, perm, preferred_element_type=F32).astype(BF16)
         p_rings[date].begin()
 
-    for piece, (low, high) in enumerate(groups):
-        for d in near[max(low, 1) : high]:
-            for kind in range(2):
-                z_copy(kind, d).wait_recv()
-        for d in (2, 1, XS - 1):
-            for kind in range(2):
-                x_copy(kind, d, piece, x).start()
-
     sets = XS * SETS
     macc[...] = jnp.zeros_like(macc)
 
-    def form(owner):
-        @pl.loop(0, zs)
+    def form(owner, piece):
+        low, high = groups[piece]
+
+        @pl.loop(low, high)
         def _(at):
             columns = pl.ds(pl.multiple_of(at * trades, trades), trades)
             key = keys[owner, at]
@@ -309,22 +303,34 @@
                 axis=0,
             ).astype(BF16)
 
-        macc[...] += lax.dot_general(spread[...], marks[...], NT, preferred_element_type=F32)
-
-    def form_from(d):
+        columns = pl.ds(low * trades, (high - low) * trades)
+        macc[...] += lax.dot_general(
+            spread[:, columns], marks[:, columns], NT, preferred_element_type=F32
+        )
+
+    def form_from(d, piece):
         from_x = lax.rem(x - d + XS, XS)
-        for piece in range(2):
+        for kind in range(2):
+            x_copy(kind, d, piece, from_x).wait_recv()
+        form(from_x, piece)
+
+    for piece, (low, high) in enumerate(groups):
+        for d in near[max(low, 1) : high]:
             for kind in range(2):
-                x_copy(kind, d, piece, from_x).wait_recv()
-        form(from_x)
-
-    form(x)
-    for ring in p_rings:
-        ring.step(1)
-    form_from(1)
-    form_from(XS - 1)
-    p_rings[0].step(2)
-    form_from(2)
+                z_copy(kind, d).wait_recv()
+        for d in (2, 1, XS - 1):
+            for kind in range(2):
+                x_copy(kind, d, piece, x).start()
+        if piece == 1:
+            p_rings[0].step(1)
+        form(x, piece)
+    form_from(1, 0)
+    form_from(XS - 1, 0)
+    form_from(2, 0)
+    p_rings[1].step(1)
+    form_from(1, 1)
+    form_from(XS - 1, 1)
+    form_from(2, 1)
     mg[scen] = macc[...].astype(BF16)
 
     cut_tall = macc.shape[0] // M_CUTS
@@ -371,9 +377,10 @@
     m_ring.begin()
     for piece in range(M_CUTS):
         pass_on(0, 0, piece)
+    p_rings[0].step(2)
     p_rings[1].step(2)
+    m_ring.step(2, pass_on)
     p_rings[0].step(3)
-    m_ring.step(2, pass_on)
     m_ring.step(1, pass_on)
     p_rings[1].step(3)
     m_ring.step(3, pass_on)
@@ -416,9 +423,13 @@
         expo[date] = jnp.maximum(total, 0.0)
 
     both = jnp.concatenate([expo[date] for date in range(DATES)], axis=0)
-    ones = jnp.ones((8, rows), F32)
+    high = both.astype(BF16)
+    low = (both - high.astype(F32)).astype(BF16)
     row = lax.dot_general(
-        ones, both, NT, precision=lax.Precision.HIGHEST, preferred_element_type=F32
+        jnp.ones((8, 2 * rows), BF16),
+        jnp.concatenate([high, low], axis=1),
+        NT,
+        preferred_element_type=F32,
     )
     sums[0] = row[0:1]
 

time: 58.5 us -> 56.6 us (0.968)
  Pallas kernels: 55.5 us -> 53.7 us
    pallas_call x1, Pallas kernels: 55.5 us -> 53.7 us  [body(): pl.pallas_call(functools.partial(kernel, fac_n, scen_n), out_shape=(jax.S...]
where the time goes in v4:
time: 56.6 us; the launch traced here: 56.5 us
  Pallas kernels  53.7 us (95%)
  local copies, waits for them, and re-layouts  2.13 us (4%)
  between operations  0.65 us (1%)
    pallas_call x1, Pallas kernels, body(): pl.pallas_call(functools.partial(kernel, fac_n, scen_n), out_shape=(jax.S...  53.7 us
    unnamed x4, local copies, waits for them, and re-layouts  2.13 us

profile of v4, /device:TPU:1, one launch (start us, length us, event | category | flops | bytes accessed | tf_op | source)
XLA Modules:
  0.0 56.5 jit_solution(15894841554025213408)
XLA Ops:
  0.6 53.7 %shard_map.122 = (f32[2,64,256]{2,1,0:T(8,128)}, f32[2,64]{1,0:T(2,128)}) custom-call(bf16[2,256,256]{2,1,0:T(8,128)(2,1)} %refs_0_.1, bf16[256,256]{1,0:T(8,128)(2,1)} %refs_1_.1, f32[1,256]{1,0:T(1,128)} %bitcast.8, s32[2,256,256]{2,1,0:T(8,128)} %refs_3_.1, bf16[2,256,256]{2,1,0:T(8,128)(2,1)} %refs_4_.1, f32[1,256]{1,0:T(1,128)} %bitcast.9, ...), custom_call_target="tpu_custom_call" | custom-call | tf_op jit(solution)/shard_map/pallas_call | solution.py:512
  54.3 0.0 copy-start
  54.3 1.6 %copy.15 = f32[2,64,256]{2,1,0:T(8,128)} copy(f32[2,64,256]{2,1,0:T(8,128)} %get-tuple-element.4) | data formatting | bytes 262144
  55.9 0.0 copy-done
  55.9 0.6 copy.16
Async XLA Ops:
  54.3 1.6 %copy-start = (f32[2,64]{1,0:T(2,128)S(1)}, f32[2,64]{1,0:T(2,128)}, u32[]{:S(2)}) copy-start(f32[2,64]{1,0:T(2,128)} %get-tuple-element.5) | copy-start | bytes 1540

commit v5 on v4

--- a/solution.py
+++ b/solution.py
@@ -55,16 +55,16 @@
         self.copy(way, d, piece, self.hops[d]).start()
 
     def begin(self):
-        for d in range(self.last, 0, -1):
-            for piece in range(self.cuts):
+        for piece in range(self.cuts):
+            for d in range(self.last, 0, -1):
                 for way in range(2):
                     if d == self.hops[d] and piece in self.pieces(way, d):
                         self.start(way, d, piece)
 
-    def step(self, d, also=None):
+    def step(self, d, also=None, only=None):
         if d > self.last:
             return
-        for piece in range(self.cuts):
+        for piece in range(self.cuts) if only is None else (only,):
             for way in range(2):
                 if piece in self.pieces(way, d):
                     self.copy(way, d, piece, 0).wait_recv()
@@ -276,6 +276,7 @@
         p_rings[date].begin()
 
     sets = XS * SETS
+    part_sets = SETS // M_CUTS
     macc[...] = jnp.zeros_like(macc)
 
     def form(owner, piece):
@@ -285,7 +286,14 @@
         def _(at):
             columns = pl.ds(pl.multiple_of(at * trades, trades), trades)
             key = keys[owner, at]
-            line = key[:, 2 * trades : 3 * trades] - sets * z
+            net = key[:, 2 * trades : 3 * trades] - sets * z
+            line = jnp.where(
+                (net >= 0) & (net < sets),
+                lax.div(lax.rem(net, SETS), part_sets) * (XS * part_sets)
+                + lax.div(net, SETS) * part_sets
+                + lax.rem(net, part_sets),
+                -1,
+            )
             marks[:, columns] = jnp.where(
                 lax.broadcasted_iota(jnp.int32, (sets, trades), 0) == line, 1.0, 0.0
             ).astype(BF16)
@@ -324,20 +332,22 @@
         if piece == 1:
             p_rings[0].step(1)
         form(x, piece)
+    p_rings[1].step(1)
     form_from(1, 0)
     form_from(XS - 1, 0)
     form_from(2, 0)
-    p_rings[1].step(1)
+    p_rings[0].step(2)
     form_from(1, 1)
     form_from(XS - 1, 1)
+    p_rings[1].step(2)
     form_from(2, 1)
     mg[scen] = macc[...].astype(BF16)
 
-    cut_tall = macc.shape[0] // M_CUTS
+    cut_sets = sets // M_CUTS
 
     def m_view(core):
         def view(owner, piece):
-            return mg.at[owner * CORES + core, pl.ds(piece * cut_tall, cut_tall)]
+            return mg.at[owner * CORES + core, :, pl.ds(piece * cut_sets, cut_sets)]
 
         return view
 
@@ -377,50 +387,57 @@
     m_ring.begin()
     for piece in range(M_CUTS):
         pass_on(0, 0, piece)
-    p_rings[0].step(2)
-    p_rings[1].step(2)
-    m_ring.step(2, pass_on)
-    p_rings[0].step(3)
-    m_ring.step(1, pass_on)
-    p_rings[1].step(3)
-    m_ring.step(3, pass_on)
-    m_ring.step(4, pass_on)
     for ring in p_rings:
-        ring.step(4)
-    for way, d, piece in c_pieces:
-        c_copy(way, d, piece, other).wait_recv()
-
-    def r_copy(date, d, slot_at):
+        ring.step(3)
+    for piece in range(M_CUTS):
+        m_ring.step(2, pass_on, piece)
+        m_ring.step(1, pass_on, piece)
+    p_rings[0].step(4)
+
+    def r_copy(date, d, piece, to):
         return pltpu.make_async_remote_copy(
-            src_ref=part.at[date, slot_at],
-            dst_ref=back.at[date, d],
-            send_sem=r_send.at[date, d],
-            recv_sem=r_recv.at[date, d],
+            src_ref=part.at[date, piece, to],
+            dst_ref=back.at[date, piece, d],
+            send_sem=r_send.at[date, piece, d],
+            recv_sem=r_recv.at[date, piece, d],
             device_id={"fac": z * XS + lax.rem(x + d, XS)},
             device_id_type=MESH,
         )
 
     tall = local * jn
-    for date in range(DATES):
-        total = None
-        for at in range(zs):
-            term = jnp.dot(
-                pg[date, at],
-                mg[:, at * tall : (at + 1) * tall, :].reshape(scen_n * tall, sets),
-                preferred_element_type=F32,
-            )
-            total = term if total is None else total + term
-        turned = total.T.reshape(XS, SETS, rows)
-        nets[date] = turned
-        part[date] = turned.astype(BF16)
-        for d in (1, XS - 1, 2):
-            r_copy(date, d, lax.rem(x + d, XS)).start()
-    for date in range(DATES):
-        total = nets[date, x]
-        for d in (1, XS - 1, 2):
-            r_copy(date, d, 0).wait_recv()
-            total = total + back[date, d].astype(F32)
-        expo[date] = jnp.maximum(total, 0.0)
+    for piece in range(M_CUTS):
+        m_ring.step(3, pass_on, piece)
+        m_ring.step(4, pass_on, piece)
+        if piece == 0:
+            p_rings[1].step(4)
+        for way, d, at in c_pieces:
+            if at == piece:
+                c_copy(way, d, at, other).wait_recv()
+        for date in range(DATES):
+            total = None
+            for at in range(zs):
+                term = jnp.dot(
+                    pg[date, at],
+                    mg[
+                        :,
+                        at * tall : (at + 1) * tall,
+                        piece * cut_sets : (piece + 1) * cut_sets,
+                    ].reshape(scen_n * tall, cut_sets),
+                    preferred_element_type=F32,
+                )
+                total = term if total is None else total + term
+            turned = total.T.reshape(XS, part_sets, rows)
+            nets[date, piece] = turned
+            part[date, piece] = turned.astype(BF16)
+            for d in (2, 1, XS - 1):
+                r_copy(date, d, piece, lax.rem(x + d, XS)).start()
+    for piece in range(M_CUTS):
+        for date in range(DATES):
+            total = nets[date, piece, x]
+            for d in (1, XS - 1, 2):
+                r_copy(date, d, piece, 0).wait_recv()
+                total = total + back[date, piece, d].astype(F32)
+            expo[date, piece * part_sets : (piece + 1) * part_sets] = jnp.maximum(total, 0.0)
 
     both = jnp.concatenate([expo[date] for date in range(DATES)], axis=0)
     high = both.astype(BF16)
@@ -464,7 +481,8 @@
         c_copy(way, d, piece, c).wait_send()
     for date in range(DATES):
         for d in range(1, XS):
-            r_copy(date, d, 0).wait_send()
+            for piece in range(M_CUTS):
+                r_copy(date, d, piece, 0).wait_send()
     for d in range(1, scen_n):
         s_copy(d).wait_send()
 
@@ -531,9 +549,9 @@
             pltpu.VMEM((scen_n, tall, sets), BF16),
             pltpu.VMEM((rows, width), F32),
             pltpu.VMEM((DATES, zs, rows, width), BF16),
-            pltpu.VMEM((DATES, XS, SETS, rows), F32),
-            pltpu.VMEM((DATES, XS, SETS, rows), BF16),
-            pltpu.VMEM((DATES, XS, SETS, rows), BF16),
+            pltpu.VMEM((DATES, M_CUTS, XS, SETS // M_CUTS, rows), F32),
+            pltpu.VMEM((DATES, M_CUTS, XS, SETS // M_CUTS, rows), BF16),
+            pltpu.VMEM((DATES, M_CUTS, XS, SETS // M_CUTS, rows), BF16),
             pltpu.VMEM((scen_n, 1, DATES * SETS), F32),
             dma((2, zs)),
             dma((2, zs)),
@@ -545,8 +563,8 @@
             dma((2, ys // 2 + 1, M_CUTS)),
             dma((2, ys // 2 + 1, M_CUTS)),
             dma((2, ys // 2 + 1, M_CUTS)),
-            dma((DATES, XS)),
-            dma((DATES, XS)),
+            dma((DATES, M_CUTS, XS)),
+            dma((DATES, M_CUTS, XS)),
             dma((scen_n,)),
             dma((scen_n,)),
         ],

time: 56.6 us -> 61.6 us (1.088)
  Pallas kernels: 53.7 us -> 58.7 us
    pallas_call x1, Pallas kernels: 53.7 us -> 58.7 us  [body(): pl.pallas_call(functools.partial(kernel, fac_n, scen_n), out_shape=(jax.S...]
where the time goes in v5:
time: 61.6 us; the launch traced here: 61.5 us
  Pallas kernels  58.7 us (95%)
  local copies, waits for them, and re-layouts  2.13 us (3%)
  between operations  0.65 us (1%)
    pallas_call x1, Pallas kernels, body(): pl.pallas_call(functools.partial(kernel, fac_n, scen_n), out_shape=(jax.S...  58.7 us
    unnamed x4, local copies, waits for them, and re-layouts  2.13 us

profile of v5, /device:TPU:1, one launch (start us, length us, event | category | flops | bytes accessed | tf_op | source)
XLA Modules:
  0.0 61.5 jit_solution(3859144852195576047)
XLA Ops:
  0.6 58.7 %shard_map.122 = (f32[2,64,256]{2,1,0:T(8,128)}, f32[2,64]{1,0:T(2,128)}) custom-call(bf16[2,256,256]{2,1,0:T(8,128)(2,1)} %refs_0_.1, bf16[256,256]{1,0:T(8,128)(2,1)} %refs_1_.1, f32[1,256]{1,0:T(1,128)} %bitcast.8, s32[2,256,256]{2,1,0:T(8,128)} %refs_3_.1, bf16[2,256,256]{2,1,0:T(8,128)(2,1)} %refs_4_.1, f32[1,256]{1,0:T(1,128)} %bitcast.9, ...), custom_call_target="tpu_custom_call" | custom-call | tf_op jit(solution)/shard_map/pallas_call | solution.py:530
  59.3 0.0 copy-start
  59.3 1.6 %copy.15 = f32[2,64,256]{2,1,0:T(8,128)} copy(f32[2,64,256]{2,1,0:T(8,128)} %get-tuple-element.4) | data formatting | bytes 262144
  60.9 0.0 copy-done
  60.9 0.6 copy.16
Async XLA Ops:
  59.3 1.6 %copy-start = (f32[2,64]{1,0:T(2,128)S(1)}, f32[2,64]{1,0:T(2,128)}, u32[]{:S(2)}) copy-start(f32[2,64]{1,0:T(2,128)} %get-tuple-element.5) | copy-start | bytes 1540

commit v6 on v4

--- a/solution.py
+++ b/solution.py
@@ -385,8 +385,6 @@
     p_rings[1].step(3)
     m_ring.step(3, pass_on)
     m_ring.step(4, pass_on)
-    for ring in p_rings:
-        ring.step(4)
     for way, d, piece in c_pieces:
         c_copy(way, d, piece, other).wait_recv()
 
@@ -402,6 +400,7 @@
 
     tall = local * jn
     for date in range(DATES):
+        p_rings[date].step(4)
         total = None
         for at in range(zs):
             term = jnp.dot(
@@ -443,14 +442,8 @@
             device_id_type=MESH,
         )
 
-    for d in range(1, scen_n):
+    for d in sorted(range(1, scen_n), key=lambda d: -min(d, scen_n - d)):
         s_copy(d).start()
-    for d in range(1, scen_n):
-        s_copy(d).wait_recv()
-    average = jnp.sum(sums[...], axis=0) / (rows * scen_n)
-    for date in range(DATES):
-        mean[date : date + 1, :] = average[:, date * SETS : (date + 1) * SETS]
-
     for kind in range(2):
         for d in range(1, zs):
             z_copy(kind, d).wait_send()
@@ -465,6 +458,12 @@
     for date in range(DATES):
         for d in range(1, XS):
             r_copy(date, d, 0).wait_send()
+    for d in range(1, scen_n):
+        s_copy(d).wait_recv()
+    average = jnp.sum(sums[...], axis=0) / (rows * scen_n)
+    for date in range(DATES):
+        mean[date : date + 1, :] = average[:, date * SETS : (date + 1) * SETS]
+
     for d in range(1, scen_n):
         s_copy(d).wait_send()
 

time: 56.6 us -> 55.9 us (0.988)
  Pallas kernels: 53.7 us -> 53 us
    pallas_call x1, Pallas kernels: 53.7 us -> 53 us  [body(): pl.pallas_call(functools.partial(kernel, fac_n, scen_n), out_shape=(jax.S...]
where the time goes in v6:
time: 55.9 us; the launch traced here: 55.8 us
  Pallas kernels  53 us (95%)
  local copies, waits for them, and re-layouts  2.13 us (4%)
  between operations  0.65 us (1%)
    pallas_call x1, Pallas kernels, body(): pl.pallas_call(functools.partial(kernel, fac_n, scen_n), out_shape=(jax.S...  53 us
    unnamed x4, local copies, waits for them, and re-layouts  2.13 us

profile of v6, /device:TPU:1, one launch (start us, length us, event | category | flops | bytes accessed | tf_op | source)
XLA Modules:
  0.0 55.8 jit_solution(16375462509717816436)
XLA Ops:
  0.6 53.0 %shard_map.122 = (f32[2,64,256]{2,1,0:T(8,128)}, f32[2,64]{1,0:T(2,128)}) custom-call(bf16[2,256,256]{2,1,0:T(8,128)(2,1)} %refs_0_.1, bf16[256,256]{1,0:T(8,128)(2,1)} %refs_1_.1, f32[1,256]{1,0:T(1,128)} %bitcast.8, s32[2,256,256]{2,1,0:T(8,128)} %refs_3_.1, bf16[2,256,256]{2,1,0:T(8,128)(2,1)} %refs_4_.1, f32[1,256]{1,0:T(1,128)} %bitcast.9, ...), custom_call_target="tpu_custom_call" | custom-call | tf_op jit(solution)/shard_map/pallas_call | solution.py:511
  53.6 0.0 copy-start
  53.6 1.6 %copy.15 = f32[2,64,256]{2,1,0:T(8,128)} copy(f32[2,64,256]{2,1,0:T(8,128)} %get-tuple-element.4) | data formatting | bytes 262144
  55.2 0.0 copy-done
  55.2 0.6 %copy.16 = f32[2,64]{1,0:T(2,128)} copy(f32[2,64]{1,0:T(2,128)S(1)} %copy-done) | data formatting | bytes 1024
Async XLA Ops:
  53.6 1.6 %copy-start = (f32[2,64]{1,0:T(2,128)S(1)}, f32[2,64]{1,0:T(2,128)}, u32[]{:S(2)}) copy-start(f32[2,64]{1,0:T(2,128)} %get-tuple-element.5) | copy-start | bytes 1540

commit v7 on v6

--- a/solution.py
+++ b/solution.py
@@ -550,7 +550,7 @@
             dma((scen_n,)),
         ],
         compiler_params=pltpu.CompilerParams(
-            collective_id=0, has_side_effects=True, vmem_limit_bytes=60 * 1024 * 1024
+            collective_id=0, has_side_effects=True, vmem_limit_bytes=55040 * 1024
         ),
     )(*arrays)
 

time: 55.9 us -> 55.1 us (0.986)
  Pallas kernels: 53 us -> 52.3 us
    pallas_call x1, Pallas kernels: 53 us -> 52.3 us  [body(): pl.pallas_call(functools.partial(kernel, fac_n, scen_n), out_shape=(jax.S...]
    unnamed x4 -> x14, local copies, waits for them, and re-layouts: 2.13 us -> 1.92 us
where the time goes in v7:
time: 55.1 us; the launch traced here: 54.9 us
  Pallas kernels  52.3 us (95%)
  local copies, waits for them, and re-layouts  1.92 us (3%)
  between operations  0.69 us (1%)
    pallas_call x1, Pallas kernels, body(): pl.pallas_call(functools.partial(kernel, fac_n, scen_n), out_shape=(jax.S...  52.3 us
    unnamed x14, local copies, waits for them, and re-layouts  1.92 us

profile of v7, /device:TPU:1, one launch (start us, length us, event | category | flops | bytes accessed | tf_op | source)
XLA Modules:
  0.0 54.9 jit_solution(7441901809775692602)
XLA Ops:
  0.6 0.0 copy-start.4
  0.6 0.0 copy-start.2
  0.7 0.0 copy-start.3
  0.7 0.0 copy-start
  0.7 0.0 copy-start.1
  0.7 0.0 copy-start.5
  0.7 0.6 %copy-done.4 = s32[256]{0:T(256)S(1)} copy-done((s32[256]{0:T(256)S(1)}, s32[256]{0:T(256)}, u32[]{:S(2)}) %copy-start.4) | copy-done | bytes 1048
  1.3 0.0 copy-done.2
  1.3 0.0 copy-done.3
  1.3 0.0 copy-done
  1.4 0.0 copy-done.1
  1.4 0.0 copy-done.5
  1.4 52.3 %shard_map.122 = (f32[2,64,256]{2,1,0:T(8,128)S(1)}, f32[2,64]{1,0:T(2,128)S(1)}) custom-call(bf16[2,256,256]{2,1,0:T(8,128)(2,1)} %refs_0_.1, bf16[256,256]{1,0:T(8,128)(2,1)} %refs_1_.1, f32[1,256]{1,0:T(1,128)S(1)} %bitcast.7, s32[2,256,256]{2,1,0:T(8,128)} %refs_3_.1, bf16[2,256,256]{2,1,0:T(8,128)(2,1)} %refs_4_.1, f32[1,256]{1,0:T(1,128)S(1)} %bitcast.8, ...), custom_call_target="tpu_custom_call" | custom-call | tf_op jit(solution)/shard_map/pallas_call | solution.py:511
  53.7 0.7 %copy.15 = f32[2,64,256]{2,1,0:T(8,128)} copy(f32[2,64,256]{2,1,0:T(8,128)S(1)} %get-tuple-element.4) | data formatting | bytes 262144
  54.4 0.6 %copy.16 = f32[2,64]{1,0:T(2,128)} copy(f32[2,64]{1,0:T(2,128)S(1)} %get-tuple-element.5) | data formatting | bytes 1024
Async XLA Ops:
  0.6 0.7 %copy-start.4 = (s32[256]{0:T(256)S(1)}, s32[256]{0:T(256)}, u32[]{:S(2)}) copy-start(s32[256]{0:T(256)} %param.21) | copy-start | bytes 3076
  0.6 0.7 %copy-start.2 = (f32[256]{0:T(256)S(1)}, f32[256]{0:T(256)}, u32[]{:S(2)}) copy-start(f32[256]{0:T(256)} %param.16) | copy-start | bytes 3076
  0.7 0.7 %copy-start.3 = (f32[256]{0:T(256)S(1)}, f32[256]{0:T(256)}, u32[]{:S(2)}) copy-start(f32[256]{0:T(256)} %param.17) | copy-start | bytes 3076
  0.7 0.7 %copy-start = (s32[256,2]{0,1:T(2,128)S(1)}, s32[256,2]{0,1:T(2,128)}, u32[]{:S(2)}) copy-start(s32[256,2]{0,1:T(2,128)} %param.18) | copy-start | bytes 6148
  0.7 0.7 %copy-start.1 = (f32[256]{0:T(256)S(1)}, f32[256]{0:T(256)}, u32[]{:S(2)}) copy-start(f32[256]{0:T(256)} %param.13) | copy-start | bytes 3076
  0.7 0.7 %copy-start.5 = (s32[64]{0:T(128)S(1)}, s32[64]{0:T(128)}, u32[]{:S(2)}) copy-start(s32[64]{0:T(128)} %refs_8_.1) | copy-start | bytes 772

commit v8 on v7

--- a/solution.py
+++ b/solution.py
@@ -222,6 +222,13 @@
             device_id_type=MESH,
         )
 
+    col_q = lax.broadcasted_iota(jnp.int32, (width, width), 1)
+    col_f = (
+        lax.rem(lax.div(col_q, jn), local) * BLOCK
+        + lax.div(col_q, jn * local) * jn
+        + lax.rem(col_q, jn)
+    )
+    perm = (lax.broadcasted_iota(jnp.int32, (width, width), 0) == col_f).astype(F32).astype(BF16)
     pl.semaphore_wait(barrier, partners)
     for d in near[:0:-1]:
         for kind in range(2):
@@ -250,13 +257,6 @@
             )
         )
 
-    col_q = lax.broadcasted_iota(jnp.int32, (width, width), 1)
-    col_f = (
-        lax.rem(lax.div(col_q, jn), local) * BLOCK
-        + lax.div(col_q, jn * local) * jn
-        + lax.rem(col_q, jn)
-    )
-    perm = (lax.broadcasted_iota(jnp.int32, (width, width), 0) == col_f).astype(F32).astype(BF16)
     v = vol[...]
     drift = 0.5 * v * v
     for date in range(DATES):
@@ -414,23 +414,25 @@
         part[date] = turned.astype(BF16)
         for d in (1, XS - 1, 2):
             r_copy(date, d, lax.rem(x + d, XS)).start()
+    totals = []
     for date in range(DATES):
         total = nets[date, x]
         for d in (1, XS - 1, 2):
             r_copy(date, d, 0).wait_recv()
             total = total + back[date, d].astype(F32)
-        expo[date] = jnp.maximum(total, 0.0)
-
-    both = jnp.concatenate([expo[date] for date in range(DATES)], axis=0)
-    high = both.astype(BF16)
-    low = (both - high.astype(F32)).astype(BF16)
-    row = lax.dot_general(
-        jnp.ones((8, 2 * rows), BF16),
-        jnp.concatenate([high, low], axis=1),
-        NT,
-        preferred_element_type=F32,
-    )
-    sums[0] = row[0:1]
+        total = jnp.maximum(total, 0.0)
+        expo[date] = total
+        high = total.astype(BF16)
+        low = (total - high.astype(F32)).astype(BF16)
+        row = lax.dot_general(
+            jnp.ones((8, 2 * rows), BF16),
+            jnp.concatenate([high, low], axis=1),
+            NT,
+            preferred_element_type=F32,
+        )
+        totals.append(row[0:1])
+
+    sums[0] = jnp.concatenate(totals, axis=1)
 
     def s_copy(d):
         return pltpu.make_async_remote_copy(

time: 55.1 us -> 55.1 us (level)
  no operation moved by 1% of the time
where the time goes in v8:
time: 55.1 us; the launch traced here: 55 us
  Pallas kernels  52.4 us (95%)
  local copies, waits for them, and re-layouts  1.92 us (3%)
  between operations  0.69 us (1%)
    pallas_call x1, Pallas kernels, body(): pl.pallas_call(functools.partial(kernel, fac_n, scen_n), out_shape=(jax.S...  52.4 us
    unnamed x14, local copies, waits for them, and re-layouts  1.92 us

profile of v8, /device:TPU:1, one launch (start us, length us, event | category | flops | bytes accessed | tf_op | source)
XLA Modules:
  0.0 55.0 jit_solution(18051264310703582327)
XLA Ops:
  0.6 0.0 copy-start.4
  0.6 0.0 copy-start.2
  0.7 0.0 copy-start.3
  0.7 0.0 copy-start
  0.7 0.0 copy-start.1
  0.7 0.0 copy-start.5
  0.7 0.6 %copy-done.4 = s32[256]{0:T(256)S(1)} copy-done((s32[256]{0:T(256)S(1)}, s32[256]{0:T(256)}, u32[]{:S(2)}) %copy-start.4) | copy-done | bytes 1048
  1.3 0.0 copy-done.2
  1.3 0.0 copy-done.3
  1.3 0.0 copy-done
  1.4 0.0 copy-done.1
  1.4 0.0 copy-done.5
  1.4 52.4 %shard_map.122 = (f32[2,64,256]{2,1,0:T(8,128)S(1)}, f32[2,64]{1,0:T(2,128)S(1)}) custom-call(bf16[2,256,256]{2,1,0:T(8,128)(2,1)} %refs_0_.1, bf16[256,256]{1,0:T(8,128)(2,1)} %refs_1_.1, f32[1,256]{1,0:T(1,128)S(1)} %bitcast.7, s32[2,256,256]{2,1,0:T(8,128)} %refs_3_.1, bf16[2,256,256]{2,1,0:T(8,128)(2,1)} %refs_4_.1, f32[1,256]{1,0:T(1,128)S(1)} %bitcast.8, ...), custom_call_target="tpu_custom_call" | custom-call | tf_op jit(solution)/shard_map/pallas_call | solution.py:513
  53.8 0.7 %copy.15 = f32[2,64,256]{2,1,0:T(8,128)} copy(f32[2,64,256]{2,1,0:T(8,128)S(1)} %get-tuple-element.4) | data formatting | bytes 262144
  54.4 0.6 %copy.16 = f32[2,64]{1,0:T(2,128)} copy(f32[2,64]{1,0:T(2,128)S(1)} %get-tuple-element.5) | data formatting | bytes 1024
Async XLA Ops:
  0.6 0.7 %copy-start.4 = (s32[256]{0:T(256)S(1)}, s32[256]{0:T(256)}, u32[]{:S(2)}) copy-start(s32[256]{0:T(256)} %param.21) | copy-start | bytes 3076
  0.6 0.7 %copy-start.2 = (f32[256]{0:T(256)S(1)}, f32[256]{0:T(256)}, u32[]{:S(2)}) copy-start(f32[256]{0:T(256)} %param.16) | copy-start | bytes 3076
  0.7 0.7 %copy-start.3 = (f32[256]{0:T(256)S(1)}, f32[256]{0:T(256)}, u32[]{:S(2)}) copy-start(f32[256]{0:T(256)} %param.17) | copy-start | bytes 3076
  0.7 0.7 %copy-start = (s32[256,2]{0,1:T(2,128)S(1)}, s32[256,2]{0,1:T(2,128)}, u32[]{:S(2)}) copy-start(s32[256,2]{0,1:T(2,128)} %param.18) | copy-start | bytes 6148
  0.7 0.7 %copy-start.1 = (f32[256]{0:T(256)S(1)}, f32[256]{0:T(256)}, u32[]{:S(2)}) copy-start(f32[256]{0:T(256)} %param.13) | copy-start | bytes 3076
  0.7 0.7 %copy-start.5 = (s32[64]{0:T(128)S(1)}, s32[64]{0:T(128)}, u32[]{:S(2)}) copy-start(s32[64]{0:T(128)} %refs_8_.1) | copy-start | bytes 772
